TPU v7x, 128 devices: a whole 4x4x4 slice. The times are simulated.
128 devices in a mesh: rows: 16 (over y, z), feat: 8 (over x, core).
Axes of the slice: x: 4, y: 4, z: 4, core: 2. Of those that a mesh axis runs over, the one named last changes fastest.
Arguments:
- features: bfloat16 [32768, 1024], P('rows', 'feat'), may hold values from -6 to 6
- tiles: bfloat16 [10240, 128, 128], P('rows'), may hold values from -0.078125 to 0.078125
- tile_row: int32 [10240], P('rows'), may hold values from 0 to 15, as said below
- tile_panel: int32 [10240], P('rows'), may hold values from 0 to 15
- tile_slot: int32 [10240], P('rows'), may hold values from 0 to 7
- counts: int32 [16], P('rows'), may hold values from 1 to 640, as said below
- need_list: int32 [16, 16, 8], replicated, may hold values from 0 to 15, as said below
- weight: bfloat16 [1024, 1024], replicated, may hold values from -0.1875 to 0.1875
Outputs:
- activations: bfloat16 [32768, 1024], P(('rows', 'feat'))
Inputs may be any that keep to these rules, and one draw needn't show every extreme that they name: need_list[g, p] holds 8 distinct tile rows of panel p. Within a row group the slots name distinct (tile_row, tile_panel, tile_slot) triples. `counts`: some row group lists exactly 640 tiles.
All inputs are finite; a program needn't handle non-finite values.
Results may differ from a plain program's by a relative error of at most 0.0049.
Values may be sent and summed in bfloat16 or wider, within the bound.
A program may use at most 128 MiB of HBM per device.

v0:
```python
import math
import jax
import jax.numpy as jnp
from jax import lax
from jax.sharding import PartitionSpec as P

TILE = 128
TPP = 16
NEED = 8


def aggregate(source, block_ids, tiles, tile_row, live_slot, shard_width):
    slots = tiles.shape[0]
    per_step = math.gcd(slots, 128)
    steps_count = slots // per_step
    blocks = source.reshape(-1, TILE, shard_width)

    def one_step(total, inputs):
        tile_part, id_part, row_part, live_part = inputs
        fetched = jnp.take(blocks, id_part, axis=0)
        product = jnp.einsum("sij,sjh->sih", tile_part, fetched, preferred_element_type=jnp.float32)
        product = jnp.where(live_part[:, None, None], product, 0.0)
        return (total.at[row_part].add(product), None)

    initial = jnp.zeros((TPP, TILE, shard_width), jnp.float32)
    total, unused = lax.scan(
        one_step,
        initial,
        (
            tiles.reshape(steps_count, per_step, TILE, TILE),
            block_ids.reshape(steps_count, per_step),
            tile_row.reshape(steps_count, per_step),
            live_slot.reshape(steps_count, per_step),
        ),
    )
    return total.reshape(TPP * TILE, shard_width)


def per_device(features, tiles, tile_row, tile_panel, tile_slot, counts, need_list, weight):
    shard_width = features.shape[1]
    groups = lax.axis_size("rows")
    own_group = lax.axis_index("rows")
    live_slot = lax.broadcasted_iota(jnp.int32, tile_row.shape, 0) < counts[0]
    source = lax.all_gather(features, "rows", axis=0, tiled=True)
    own_table = lax.dynamic_index_in_dim(need_list, own_group, 0, keepdims=False).reshape(-1)
    flat_index = tile_panel * NEED + tile_slot
    matches = flat_index[:, None] == lax.broadcasted_iota(jnp.int32, (1, groups * NEED), 1)
    picked = jnp.sum(jnp.where(matches, own_table[None, :], 0), axis=1)
    block_ids = tile_panel * TPP + picked
    summed = aggregate(source, block_ids, tiles, tile_row, live_slot, shard_width)
    rounded = summed.astype(jnp.bfloat16)
    rows_full = lax.all_to_all(rounded, "feat", split_axis=0, concat_axis=1, tiled=True)
    mixed = jnp.dot(rows_full, weight, preferred_element_type=jnp.float32)
    return jnp.maximum(mixed, 0.0).astype(jnp.bfloat16)


def solution(mesh):
    return jax.shard_map(
        per_device,
        mesh=mesh,
        in_specs=(
            P("rows", "feat"),
            P("rows", None, None),
            P("rows"),
            P("rows"),
            P("rows"),
            P("rows"),
            P(),
            P(),
        ),
        out_specs=P(("rows", "feat"), None),
        check_vma=False,
    )
```

profile of v0, /device:TPU:1, one launch (start us, length us, event | category | flops | bytes accessed | tf_op | source)
XLA Modules:
  0.0 267.5 jit_solution(11468187125140343390)
XLA Ops:
  6.5 0.0 copy-start
  6.5 0.0 all-gather.2.cloned.1.call-start
  6.5 0.7 all-gather.2.cloned.1.call-update
  7.3 0.7 constant_dynamic-slice_fusion.2
  8.0 0.1 copy.13
  8.0 0.1 broadcast_in_dim.45
  8.8 0.7 multiply_add_fusion
  9.5 0.3 select_reduce_fusion
  9.8 0.7 add_bitcast_fusion
  10.5 73.1 %all-gather.2.cloned.1.call-done = bf16[32768,128]{1,0:T(8,128)(2,1)} async-done(((bf16[2048,128]{1,0:T(8,128)(2,1)}), bf16[32768,128]{1,0:T(8,128)(2,1)}) %all-gather.2.cloned.1.call-update) | async-done | bytes 8388624 | tf_op jit(solution)/shard_map/all_gather | solution.py:44
  83.6 0.1 broadcast_in_dim.44
  83.7 161.1 %while.10 = (s32[]{:T(128)}, f32[16,128,128]{2,1,0:T(8,128)S(1)}, s32[5,128]{1,0:T(8,128)}, pred[5,128]{1,0:T(8,128)(4,1)S(1)}, bf16[5,128,128,128]{3,2,1,0:T(8,...) while((s32[]{:T(128)}, f32[16,128,128]{2,1,0:T(8,128)S(1)}, ...), condition=%wide.region_3.4_spmd, body=%wide.region_1.3_spmd.sunk | while | flops 543164928 | bytes 50341088 | solution.py:26
  83.7 0.7 fusion.23
  84.4 6.4 %gather_fusion = bf16[128,128,128]{2,1,0:T(8,128)(2,1)} fusion(bf16[256,128,128]{2,1,0:T(8,128)(2,1)} %get-tuple-element.128, s32[1024]{0:T(1024)S(1)} %pad_clamp_fusion.2), kind=kCustom, calls=%fused_computation.clone.1 | custom fusion | bytes 8389120 | tf_op jit(solution)/shard_map/while/body/eval_jaxpr/jit(_take)/gather | solution.py:20
  90.9 8.0 %broadcast_select_fusion.2 = f32[128,128,128]{2,1,0:T(8,128)} fusion(pred[128]{0:T(512)(128)(4,1)S(1)} %dynamic-slice_bitcast_fusion.2, bf16[128,128,128]{2,1,0:T(8,128)(2,1)} %gather_fusion, pred[128]{0:T(512)(128)(4,1)S(1)} %compare_and_fusion.2, bf16[5,128,128,128]{3,2,1,0:T(8,128)(2,1)} %get-tuple-element.126, s32[]{:T(128)} %get-tuple-element.114), kind=kOutput, calls=%fused_computation.4.clone.1 | convolution fusion | flops 541065216 | bytes 16777984 | tf_op jit(solution)/shard_map/while/body/eval_jaxpr/sij,sjh->sih/dot_general | solution.py:21
  98.9 17.0 %scatter_fusion = f32[16,128,128]{2,1,0:T(8,128)S(1)} fusion(f32[16,128,128]{2,1,0:T(8,128)S(1)} %get-tuple-element.115, s32[128]{0:T(128)S(1)} %get-tuple-element.104, f32[128,128,128]{2,1,0:T(8,128)} %broadcast_select_fusion.2), kind=kCustom, calls=%fused_computation.1.clone.1 | custom fusion | flops 2097152 | bytes 25166336 | tf_op jit(solution)/shard_map/while/body/eval_jaxpr/scatter-add | solution.py:23
  115.9 0.7 fusion.23
  116.6 6.4 %gather_fusion = bf16[128,128,128]{2,1,0:T(8,128)(2,1)} fusion(bf16[256,128,128]{2,1,0:T(8,128)(2,1)} %get-tuple-element.128, s32[1024]{0:T(1024)S(1)} %pad_clamp_fusion.2), kind=kCustom, calls=%fused_computation.clone.1 | custom fusion | bytes 8389120 | tf_op jit(solution)/shard_map/while/body/eval_jaxpr/jit(_take)/gather | solution.py:20
  123.1 8.0 %broadcast_select_fusion.2 = f32[128,128,128]{2,1,0:T(8,128)} fusion(pred[128]{0:T(512)(128)(4,1)S(1)} %dynamic-slice_bitcast_fusion.2, bf16[128,128,128]{2,1,0:T(8,128)(2,1)} %gather_fusion, pred[128]{0:T(512)(128)(4,1)S(1)} %compare_and_fusion.2, bf16[5,128,128,128]{3,2,1,0:T(8,128)(2,1)} %get-tuple-element.126, s32[]{:T(128)} %get-tuple-element.114), kind=kOutput, calls=%fused_computation.4.clone.1 | convolution fusion | flops 541065216 | bytes 16777984 | tf_op jit(solution)/shard_map/while/body/eval_jaxpr/sij,sjh->sih/dot_general | solution.py:21
  131.1 17.0 %scatter_fusion = f32[16,128,128]{2,1,0:T(8,128)S(1)} fusion(f32[16,128,128]{2,1,0:T(8,128)S(1)} %get-tuple-element.115, s32[128]{0:T(128)S(1)} %get-tuple-element.104, f32[128,128,128]{2,1,0:T(8,128)} %broadcast_select_fusion.2), kind=kCustom, calls=%fused_computation.1.clone.1 | custom fusion | flops 2097152 | bytes 25166336 | tf_op jit(solution)/shard_map/while/body/eval_jaxpr/scatter-add | solution.py:23
  148.2 0.7 fusion.23
  148.9 6.4 %gather_fusion = bf16[128,128,128]{2,1,0:T(8,128)(2,1)} fusion(bf16[256,128,128]{2,1,0:T(8,128)(2,1)} %get-tuple-element.128, s32[1024]{0:T(1024)S(1)} %pad_clamp_fusion.2), kind=kCustom, calls=%fused_computation.clone.1 | custom fusion | bytes 8389120 | tf_op jit(solution)/shard_map/while/body/eval_jaxpr/jit(_take)/gather | solution.py:20
  155.3 8.0 %broadcast_select_fusion.2 = f32[128,128,128]{2,1,0:T(8,128)} fusion(pred[128]{0:T(512)(128)(4,1)S(1)} %dynamic-slice_bitcast_fusion.2, bf16[128,128,128]{2,1,0:T(8,128)(2,1)} %gather_fusion, pred[128]{0:T(512)(128)(4,1)S(1)} %compare_and_fusion.2, bf16[5,128,128,128]{3,2,1,0:T(8,128)(2,1)} %get-tuple-element.126, s32[]{:T(128)} %get-tuple-element.114), kind=kOutput, calls=%fused_computation.4.clone.1 | convolution fusion | flops 541065216 | bytes 16777984 | tf_op jit(solution)/shard_map/while/body/eval_jaxpr/sij,sjh->sih/dot_general | solution.py:21
  163.3 17.0 %scatter_fusion = f32[16,128,128]{2,1,0:T(8,128)S(1)} fusion(f32[16,128,128]{2,1,0:T(8,128)S(1)} %get-tuple-element.115, s32[128]{0:T(128)S(1)} %get-tuple-element.104, f32[128,128,128]{2,1,0:T(8,128)} %broadcast_select_fusion.2), kind=kCustom, calls=%fused_computation.1.clone.1 | custom fusion | flops 2097152 | bytes 25166336 | tf_op jit(solution)/shard_map/while/body/eval_jaxpr/scatter-add | solution.py:23
  180.4 0.7 fusion.23
  181.1 6.4 %gather_fusion = bf16[128,128,128]{2,1,0:T(8,128)(2,1)} fusion(bf16[256,128,128]{2,1,0:T(8,128)(2,1)} %get-tuple-element.128, s32[1024]{0:T(1024)S(1)} %pad_clamp_fusion.2), kind=kCustom, calls=%fused_computation.clone.1 | custom fusion | bytes 8389120 | tf_op jit(solution)/shard_map/while/body/eval_jaxpr/jit(_take)/gather | solution.py:20
  187.5 8.0 %broadcast_select_fusion.2 = f32[128,128,128]{2,1,0:T(8,128)} fusion(pred[128]{0:T(512)(128)(4,1)S(1)} %dynamic-slice_bitcast_fusion.2, bf16[128,128,128]{2,1,0:T(8,128)(2,1)} %gather_fusion, pred[128]{0:T(512)(128)(4,1)S(1)} %compare_and_fusion.2, bf16[5,128,128,128]{3,2,1,0:T(8,128)(2,1)} %get-tuple-element.126, s32[]{:T(128)} %get-tuple-element.114), kind=kOutput, calls=%fused_computation.4.clone.1 | convolution fusion | flops 541065216 | bytes 16777984 | tf_op jit(solution)/shard_map/while/body/eval_jaxpr/sij,sjh->sih/dot_general | solution.py:21
  195.5 17.0 %scatter_fusion = f32[16,128,128]{2,1,0:T(8,128)S(1)} fusion(f32[16,128,128]{2,1,0:T(8,128)S(1)} %get-tuple-element.115, s32[128]{0:T(128)S(1)} %get-tuple-element.104, f32[128,128,128]{2,1,0:T(8,128)} %broadcast_select_fusion.2), kind=kCustom, calls=%fused_computation.1.clone.1 | custom fusion | flops 2097152 | bytes 25166336 | tf_op jit(solution)/shard_map/while/body/eval_jaxpr/scatter-add | solution.py:23
  212.6 0.7 fusion.23
  213.3 6.4 %gather_fusion = bf16[128,128,128]{2,1,0:T(8,128)(2,1)} fusion(bf16[256,128,128]{2,1,0:T(8,128)(2,1)} %get-tuple-element.128, s32[1024]{0:T(1024)S(1)} %pad_clamp_fusion.2), kind=kCustom, calls=%fused_computation.clone.1 | custom fusion | bytes 8389120 | tf_op jit(solution)/shard_map/while/body/eval_jaxpr/jit(_take)/gather | solution.py:20
  219.7 8.0 %broadcast_select_fusion.2 = f32[128,128,128]{2,1,0:T(8,128)} fusion(pred[128]{0:T(512)(128)(4,1)S(1)} %dynamic-slice_bitcast_fusion.2, bf16[128,128,128]{2,1,0:T(8,128)(2,1)} %gather_fusion, pred[128]{0:T(512)(128)(4,1)S(1)} %compare_and_fusion.2, bf16[5,128,128,128]{3,2,1,0:T(8,128)(2,1)} %get-tuple-element.126, s32[]{:T(128)} %get-tuple-element.114), kind=kOutput, calls=%fused_computation.4.clone.1 | convolution fusion | flops 541065216 | bytes 16777984 | tf_op jit(solution)/shard_map/while/body/eval_jaxpr/sij,sjh->sih/dot_general | solution.py:21
  227.7 17.0 %scatter_fusion = f32[16,128,128]{2,1,0:T(8,128)S(1)} fusion(f32[16,128,128]{2,1,0:T(8,128)S(1)} %get-tuple-element.115, s32[128]{0:T(128)S(1)} %get-tuple-element.104, f32[128,128,128]{2,1,0:T(8,128)} %broadcast_select_fusion.2), kind=kCustom, calls=%fused_computation.1.clone.1 | custom fusion | flops 2097152 | bytes 25166336 | tf_op jit(solution)/shard_map/while/body/eval_jaxpr/scatter-add | solution.py:23
  244.8 0.1 convert_element_type.10
  244.9 14.1 %all_to_all.16 = bf16[8,256,128]{2,1,0:T(8,128)(2,1)S(1)} all-to-all(bf16[8,256,128]{2,1,0:T(8,128)(2,1)S(1)} %bitcast.45), channel_id=1, replica_groups=mesh['rows'=16,'feat'=8] {'feat'}, dimensions={0} | all-to-all | bytes 1048576 | tf_op jit(solution)/shard_map/all_to_all | solution.py:52
  259.0 0.2 copy.14
  259.2 0.0 copy-done
  259.2 1.5 fusion.15
  (16 shorter events, 0.2 us)
Async XLA Ops:
  6.5 252.6 %copy-start = (bf16[1024,1024]{1,0:T(8,128)(2,1)S(1)}, bf16[1024,1024]{1,0:T(8,128)(2,1)}, u32[]{:S(2)}) copy-start(bf16[1024,1024]{1,0:T(8,128)(2,1)} %param.17) | copy-start | bytes 6291460
  6.5 77.1 %all-gather.2.cloned.1.call-start = ((), (), s32[]{:S(2)}) async-start(), calls=%async_computation.1 | async-start | bytes 8912896 | tf_op jit(solution)/shard_map/all_gather | solution.py:44
Sparse Core Ops, SparseCore 0:
  9.5 74.0 all-gather.1
where the time goes:
time: 270 us; the launch traced here: 268 us
  other arithmetic  90.5 us (34%)
  waiting for transfers between devices  73.9 us (27%)
  matrix products  41.6 us (15%)
  local copies, waits for them, and re-layouts  33.2 us (12%)
  blocking collectives  14.1 us (5%)
  between operations  14.1 us (5%)
    scatter-add x5, other arithmetic, one_step(): return (total.at[row_part].add(product), None)  85.2 us
    all_gather x1, waiting for transfers between devices, per_device(): source = lax.all_gather(features, 'rows', axis=0, tiled=True)  73.1 us
    dot_general x5, matrix products, one_step(): jnp.einsum('sij,sjh->sih', tile_part, fetched, preferred_element_type=jnp...  40.1 us
    gather x5, local copies, waits for them, and re-layouts, one_step(): fetched = jnp.take(blocks, id_part, axis=0)  32 us
    all_to_all x1, blocking collectives, per_device(): lax.all_to_all(rounded, 'feat', split_axis=0, concat_axis=1, tiled=True)  14.1 us
  transfers between devices with their start and end apart: 1, of which 1 were waited for; matrix products, arithmetic and copies ran while one was open for 1% of the time, Pallas kernels for 0%

commit v1 on v0

--- a/solution.py
+++ b/solution.py
@@ -41,7 +41,9 @@
     groups = lax.axis_size("rows")
     own_group = lax.axis_index("rows")
     live_slot = lax.broadcasted_iota(jnp.int32, tile_row.shape, 0) < counts[0]
-    source = lax.all_gather(features, "rows", axis=0, tiled=True)
+    source = jnp.concatenate(
+        lax.all_to_all(jnp.stack([features] * lax.axis_size("rows")), "rows", 0, 0), axis=0
+    )
     own_table = lax.dynamic_index_in_dim(need_list, own_group, 0, keepdims=False).reshape(-1)
     flat_index = tile_panel * NEED + tile_slot
     matches = flat_index[:, None] == lax.broadcasted_iota(jnp.int32, (1, groups * NEED), 1)

time: 270 us -> 342 us (1.27)
  waiting for transfers between devices: 73.9 us -> 144 us
  between operations: 14.1 us -> 0.75 us
  starting transfers between devices: 0.01 us -> 8.78 us
  local copies, waits for them, and re-layouts: 33.2 us -> 39.2 us
    all_to_all x0 -> x1, waiting for transfers between devices: none -> 144 us  [per_device(): lax.all_to_all(jnp.stack([features] * lax.axis_size('rows')), 'rows', 0, 0)]
    all_gather x1 -> x0, waiting for transfers between devices: 73.1 us -> none  [per_device(): source = lax.all_gather(features, 'rows', axis=0, tiled=True)]
    all_to_all x0 -> x1, starting transfers between devices: none -> 8.78 us  [per_device(): lax.all_to_all(jnp.stack([features] * lax.axis_size('rows')), 'rows', 0, 0)]
    another operation x0 -> x1, local copies, waits for them, and re-layouts: none -> 6.02 us  [per_device(): jnp.stack([features] * lax.axis_size('rows'))]
  transfers between devices with their start and end apart: 1 -> 1, of which waited for: 1 -> 1; matrix products, arithmetic and copies ran while one was open for 1% -> 0% of each run, Pallas kernels for 0% -> 0%
where the time goes in v1:
time: 342 us; the launch traced here: 340 us
  waiting for transfers between devices  144 us (42%)
  other arithmetic  89.1 us (26%)
  matrix products  41.6 us (12%)
  local copies, waits for them, and re-layouts  39.2 us (11%)
  blocking collectives  15.9 us (5%)
  starting transfers between devices  8.78 us (3%)
    all_to_all x1, waiting for transfers between devices, per_device(): lax.all_to_all(jnp.stack([features] * lax.axis_size('rows')), 'rows', 0, 0)  144 us
    scatter-add x5, other arithmetic, one_step(): return (total.at[row_part].add(product), None)  85.2 us
    dot_general x5, matrix products, one_step(): jnp.einsum('sij,sjh->sih', tile_part, fetched, preferred_element_type=jnp...  40.1 us
    gather x5, local copies, waits for them, and re-layouts, one_step(): fetched = jnp.take(blocks, id_part, axis=0)  32 us
    all_to_all x1, blocking collectives, per_device(): lax.all_to_all(rounded, 'feat', split_axis=0, concat_axis=1, tiled=True)  15.9 us
    all_to_all x1, starting transfers between devices, per_device(): lax.all_to_all(jnp.stack([features] * lax.axis_size('rows')), 'rows', 0, 0)  8.78 us
  transfers between devices with their start and end apart: 1, of which 1 were waited for; matrix products, arithmetic and copies ran while one was open for 0% of the time, Pallas kernels for 0%

profile of v1, /device:TPU:1, one launch (start us, length us, event | category | flops | bytes accessed | tf_op | source)
XLA Modules:
  0.0 339.9 jit_solution(7895871420069625294)
XLA Ops:
  0.0 0.0 copy-start
  0.0 6.0 %stack.2 = bf16[16,2048,128]{2,1,0:T(8,128)(2,1)} broadcast(bf16[2048,128]{1,0:T(8,128)(2,1)} %param.10), dimensions={1,2} | broadcast | bytes 8912896 | tf_op jit(solution)/shard_map/stack | solution.py:45
  6.0 0.0 copy-start.1
  6.0 0.0 copy-start.2
  6.0 8.8 %all-to-all-start = ((bf16[16,2048,128]{2,1,0:T(8,128)(2,1)}), bf16[16,2048,128]{2,1,0:T(8,128)(2,1)}, u32[]{:S(2)}, u32[]{:S(2)}) async-start(bf16[16,2048,128]{2,1,0:T(8,128)(2,1)} %stack.2), calls=%async_computation | async-start | bytes 16777216 | tf_op jit(solution)/shard_map/all_to_all | solution.py:45
  14.8 0.7 constant_dynamic-slice_fusion.2
  15.5 0.1 copy.13
  15.6 0.1 broadcast_in_dim.45
  16.3 0.0 copy-done.1
  16.4 0.0 copy-done.2
  16.4 0.3 select_reduce_fusion
  16.7 144.3 %all-to-all-done = bf16[16,2048,128]{2,1,0:T(8,128)(2,1)} async-done(((bf16[16,2048,128]{2,1,0:T(8,128)(2,1)}), bf16[16,2048,128]{2,1,0:T(8,128)(2,1)}, u32[]{:S(2)}, u32[]{:S(2)}) %all-to-all-start) | async-done | bytes 8388640 | tf_op jit(solution)/shard_map/all_to_all | solution.py:45
  161.0 0.1 broadcast_in_dim.44
  161.1 161.1 %while.10 = (s32[]{:T(128)}, f32[16,128,128]{2,1,0:T(8,128)S(1)}, s32[5,128]{1,0:T(8,128)}, pred[5,128]{1,0:T(8,128)(4,1)S(1)}, bf16[5,128,128,128]{3,2,1,0:T(8,...) while((s32[]{:T(128)}, f32[16,128,128]{2,1,0:T(8,128)S(1)}, ...), condition=%wide.region_3.4_spmd, body=%wide.region_1.3_spmd.sunk | while | flops 543164928 | bytes 50341088 | solution.py:26
  161.1 0.7 fusion.23
  161.8 6.4 %gather_fusion = bf16[128,128,128]{2,1,0:T(8,128)(2,1)} fusion(bf16[256,128,128]{2,1,0:T(8,128)(2,1)} %get-tuple-element.128, s32[1024]{0:T(1024)S(1)} %pad_clamp_fusion.2), kind=kCustom, calls=%fused_computation.clone.1 | custom fusion | bytes 8389120 | tf_op jit(solution)/shard_map/while/body/eval_jaxpr/jit(_take)/gather | solution.py:20
  168.2 8.0 %broadcast_select_fusion.2 = f32[128,128,128]{2,1,0:T(8,128)} fusion(pred[128]{0:T(512)(128)(4,1)S(1)} %dynamic-slice_bitcast_fusion.2, bf16[128,128,128]{2,1,0:T(8,128)(2,1)} %gather_fusion, pred[128]{0:T(512)(128)(4,1)S(1)} %compare_and_fusion.2, bf16[5,128,128,128]{3,2,1,0:T(8,128)(2,1)} %get-tuple-element.126, s32[]{:T(128)} %get-tuple-element.114), kind=kOutput, calls=%fused_computation.4.clone.1 | convolution fusion | flops 541065216 | bytes 16777984 | tf_op jit(solution)/shard_map/while/body/eval_jaxpr/sij,sjh->sih/dot_general | solution.py:21
  176.2 17.0 %scatter_fusion = f32[16,128,128]{2,1,0:T(8,128)S(1)} fusion(f32[16,128,128]{2,1,0:T(8,128)S(1)} %get-tuple-element.115, s32[128]{0:T(128)S(1)} %get-tuple-element.104, f32[128,128,128]{2,1,0:T(8,128)} %broadcast_select_fusion.2), kind=kCustom, calls=%fused_computation.1.clone.1 | custom fusion | flops 2097152 | bytes 25166336 | tf_op jit(solution)/shard_map/while/body/eval_jaxpr/scatter-add | solution.py:23
  193.3 0.7 fusion.23
  194.0 6.4 %gather_fusion = bf16[128,128,128]{2,1,0:T(8,128)(2,1)} fusion(bf16[256,128,128]{2,1,0:T(8,128)(2,1)} %get-tuple-element.128, s32[1024]{0:T(1024)S(1)} %pad_clamp_fusion.2), kind=kCustom, calls=%fused_computation.clone.1 | custom fusion | bytes 8389120 | tf_op jit(solution)/shard_map/while/body/eval_jaxpr/jit(_take)/gather | solution.py:20
  200.4 8.0 %broadcast_select_fusion.2 = f32[128,128,128]{2,1,0:T(8,128)} fusion(pred[128]{0:T(512)(128)(4,1)S(1)} %dynamic-slice_bitcast_fusion.2, bf16[128,128,128]{2,1,0:T(8,128)(2,1)} %gather_fusion, pred[128]{0:T(512)(128)(4,1)S(1)} %compare_and_fusion.2, bf16[5,128,128,128]{3,2,1,0:T(8,128)(2,1)} %get-tuple-element.126, s32[]{:T(128)} %get-tuple-element.114), kind=kOutput, calls=%fused_computation.4.clone.1 | convolution fusion | flops 541065216 | bytes 16777984 | tf_op jit(solution)/shard_map/while/body/eval_jaxpr/sij,sjh->sih/dot_general | solution.py:21
  208.4 17.0 %scatter_fusion = f32[16,128,128]{2,1,0:T(8,128)S(1)} fusion(f32[16,128,128]{2,1,0:T(8,128)S(1)} %get-tuple-element.115, s32[128]{0:T(128)S(1)} %get-tuple-element.104, f32[128,128,128]{2,1,0:T(8,128)} %broadcast_select_fusion.2), kind=kCustom, calls=%fused_computation.1.clone.1 | custom fusion | flops 2097152 | bytes 25166336 | tf_op jit(solution)/shard_map/while/body/eval_jaxpr/scatter-add | solution.py:23
  225.5 0.7 fusion.23
  226.2 6.4 %gather_fusion = bf16[128,128,128]{2,1,0:T(8,128)(2,1)} fusion(bf16[256,128,128]{2,1,0:T(8,128)(2,1)} %get-tuple-element.128, s32[1024]{0:T(1024)S(1)} %pad_clamp_fusion.2), kind=kCustom, calls=%fused_computation.clone.1 | custom fusion | bytes 8389120 | tf_op jit(solution)/shard_map/while/body/eval_jaxpr/jit(_take)/gather | solution.py:20
  232.6 8.0 %broadcast_select_fusion.2 = f32[128,128,128]{2,1,0:T(8,128)} fusion(pred[128]{0:T(512)(128)(4,1)S(1)} %dynamic-slice_bitcast_fusion.2, bf16[128,128,128]{2,1,0:T(8,128)(2,1)} %gather_fusion, pred[128]{0:T(512)(128)(4,1)S(1)} %compare_and_fusion.2, bf16[5,128,128,128]{3,2,1,0:T(8,128)(2,1)} %get-tuple-element.126, s32[]{:T(128)} %get-tuple-element.114), kind=kOutput, calls=%fused_computation.4.clone.1 | convolution fusion | flops 541065216 | bytes 16777984 | tf_op jit(solution)/shard_map/while/body/eval_jaxpr/sij,sjh->sih/dot_general | solution.py:21
  240.7 17.0 %scatter_fusion = f32[16,128,128]{2,1,0:T(8,128)S(1)} fusion(f32[16,128,128]{2,1,0:T(8,128)S(1)} %get-tuple-element.115, s32[128]{0:T(128)S(1)} %get-tuple-element.104, f32[128,128,128]{2,1,0:T(8,128)} %broadcast_select_fusion.2), kind=kCustom, calls=%fused_computation.1.clone.1 | custom fusion | flops 2097152 | bytes 25166336 | tf_op jit(solution)/shard_map/while/body/eval_jaxpr/scatter-add | solution.py:23
  257.7 0.7 fusion.23
  258.4 6.4 %gather_fusion = bf16[128,128,128]{2,1,0:T(8,128)(2,1)} fusion(bf16[256,128,128]{2,1,0:T(8,128)(2,1)} %get-tuple-element.128, s32[1024]{0:T(1024)S(1)} %pad_clamp_fusion.2), kind=kCustom, calls=%fused_computation.clone.1 | custom fusion | bytes 8389120 | tf_op jit(solution)/shard_map/while/body/eval_jaxpr/jit(_take)/gather | solution.py:20
  264.8 8.0 %broadcast_select_fusion.2 = f32[128,128,128]{2,1,0:T(8,128)} fusion(pred[128]{0:T(512)(128)(4,1)S(1)} %dynamic-slice_bitcast_fusion.2, bf16[128,128,128]{2,1,0:T(8,128)(2,1)} %gather_fusion, pred[128]{0:T(512)(128)(4,1)S(1)} %compare_and_fusion.2, bf16[5,128,128,128]{3,2,1,0:T(8,128)(2,1)} %get-tuple-element.126, s32[]{:T(128)} %get-tuple-element.114), kind=kOutput, calls=%fused_computation.4.clone.1 | convolution fusion | flops 541065216 | bytes 16777984 | tf_op jit(solution)/shard_map/while/body/eval_jaxpr/sij,sjh->sih/dot_general | solution.py:21
  272.9 17.0 %scatter_fusion = f32[16,128,128]{2,1,0:T(8,128)S(1)} fusion(f32[16,128,128]{2,1,0:T(8,128)S(1)} %get-tuple-element.115, s32[128]{0:T(128)S(1)} %get-tuple-element.104, f32[128,128,128]{2,1,0:T(8,128)} %broadcast_select_fusion.2), kind=kCustom, calls=%fused_computation.1.clone.1 | custom fusion | flops 2097152 | bytes 25166336 | tf_op jit(solution)/shard_map/while/body/eval_jaxpr/scatter-add | solution.py:23
  289.9 0.7 fusion.23
  290.6 6.4 %gather_fusion = bf16[128,128,128]{2,1,0:T(8,128)(2,1)} fusion(bf16[256,128,128]{2,1,0:T(8,128)(2,1)} %get-tuple-element.128, s32[1024]{0:T(1024)S(1)} %pad_clamp_fusion.2), kind=kCustom, calls=%fused_computation.clone.1 | custom fusion | bytes 8389120 | tf_op jit(solution)/shard_map/while/body/eval_jaxpr/jit(_take)/gather | solution.py:20
  297.0 8.0 %broadcast_select_fusion.2 = f32[128,128,128]{2,1,0:T(8,128)} fusion(pred[128]{0:T(512)(128)(4,1)S(1)} %dynamic-slice_bitcast_fusion.2, bf16[128,128,128]{2,1,0:T(8,128)(2,1)} %gather_fusion, pred[128]{0:T(512)(128)(4,1)S(1)} %compare_and_fusion.2, bf16[5,128,128,128]{3,2,1,0:T(8,128)(2,1)} %get-tuple-element.126, s32[]{:T(128)} %get-tuple-element.114), kind=kOutput, calls=%fused_computation.4.clone.1 | convolution fusion | flops 541065216 | bytes 16777984 | tf_op jit(solution)/shard_map/while/body/eval_jaxpr/sij,sjh->sih/dot_general | solution.py:21
  305.1 17.0 %scatter_fusion = f32[16,128,128]{2,1,0:T(8,128)S(1)} fusion(f32[16,128,128]{2,1,0:T(8,128)S(1)} %get-tuple-element.115, s32[128]{0:T(128)S(1)} %get-tuple-element.104, f32[128,128,128]{2,1,0:T(8,128)} %broadcast_select_fusion.2), kind=kCustom, calls=%fused_computation.1.clone.1 | custom fusion | flops 2097152 | bytes 25166336 | tf_op jit(solution)/shard_map/while/body/eval_jaxpr/scatter-add | solution.py:23
  322.1 0.1 convert_element_type.10
  322.2 15.9 %all_to_all.21 = bf16[8,256,128]{2,1,0:T(8,128)(2,1)S(1)} all-to-all(bf16[8,256,128]{2,1,0:T(8,128)(2,1)S(1)} %bitcast.44), channel_id=1, replica_groups=mesh['rows'=16,'feat'=8] {'feat'}, dimensions={0} | all-to-all | bytes 1048576 | tf_op jit(solution)/shard_map/all_to_all | solution.py:54
  338.1 0.2 copy.14
  338.4 0.0 copy-done
  338.4 1.5 fusion.15
  (18 shorter events, 0.2 us)
Async XLA Ops:
  0.0 338.4 %copy-start = (bf16[1024,1024]{1,0:T(8,128)(2,1)S(1)}, bf16[1024,1024]{1,0:T(8,128)(2,1)}, u32[]{:S(2)}) copy-start(bf16[1024,1024]{1,0:T(8,128)(2,1)} %param.17) | copy-start | bytes 6291460
  6.0 10.3 %copy-start.1 = (s32[640]{0:T(1024)S(1)}, s32[640]{0:T(1024)}, u32[]{:S(2)}) copy-start(s32[640]{0:T(1024)} %param.13) | copy-start | bytes 7684
  6.0 10.3 %copy-start.2 = (s32[640]{0:T(1024)S(1)}, s32[640]{0:T(1024)}, u32[]{:S(2)}) copy-start(s32[640]{0:T(1024)} %param.14) | copy-start | bytes 7684
  6.0 154.9 %all-to-all-start = ((bf16[16,2048,128]{2,1,0:T(8,128)(2,1)}), bf16[16,2048,128]{2,1,0:T(8,128)(2,1)}, u32[]{:S(2)}, u32[]{:S(2)}) async-start(bf16[16,2048,128]{2,1,0:T(8,128)(2,1)} %stack.2), calls=%async_computation | async-start | bytes 16777216 | tf_op jit(solution)/shard_map/all_to_all | solution.py:45
